TPU v7x, 32 devices: a whole 2x2x4 slice. The times are simulated.
32 devices in a mesh: span: 2 (over x), seq: 16 (over z, y, core).
Axes of the slice: x: 2, y: 2, z: 4, core: 2. Of those that a mesh axis runs over, the one named last changes fastest.
Arguments:
- queries: bfloat16 [2, 128, 2560], P('span', 'seq'), may hold values from -8 to 8
- keys: bfloat16 [2, 128, 2560], P('span', 'seq'), may hold values from -8 to 8
- values: bfloat16 [2, 128, 2560], P('span', 'seq'), may hold values from -6 to 6
- span_index: int32 [2], replicated, may hold values from 0 to 1, each once
Outputs:
- attended: bfloat16 [2, 128, 2560], P('span', 'seq')
Inputs may be any that keep to these rules, and one draw needn't show every extreme that they name: A permutation; group g denoises span span_index[g] and attends to itself and to the group holding the span before it.
All inputs are finite; a program needn't handle non-finite values.
Results may differ from a plain program's by a relative error of at most 0.015.
Values may be sent and summed in bfloat16 or wider, within the bound.
No kernel may reach another device: no remote copies, remote signals or barrier semaphores. Data moves between devices by JAX's collectives and lax.ppermute only.
A program may use at most 64 MiB of HBM per device.

v0:
```python
import functools
import math

import jax
import jax.numpy as jnp
from jax import lax
from jax.experimental import pallas as pl
from jax.experimental.pallas import tpu as pltpu
from jax.sharding import PartitionSpec as P

HEADS = 20
MASKED = -1e30
AXES = ("span", "seq")


def slot_heads(slots):
    spread = [d for d in range(slots) if d % 2 == 0] + [d for d in range(slots) if d % 2]
    heads = [0] * slots
    for place, d in enumerate(spread):
        heads[d] = place % HEADS
    return heads, spread[:HEADS]


def rank_order(groups, ranks):
    per = [r for c in range(2) for y in range(2) for r in range(ranks) if r % 4 == 2 * y + c]
    return [g * ranks + r for g in range(groups) for r in per]


def pack_kernel(heads, q_hbm, k_hbm, v_hbm, span_hbm, out_ref, bias_ref, held, spans, sems):
    copies = [
        pltpu.make_async_copy(src, held.at[pl.ds(i, 1)], sems.at[i])
        for i, src in enumerate((q_hbm, k_hbm, v_hbm))
    ]
    index = pltpu.make_async_copy(span_hbm, spans, sems.at[3])
    index.start()
    for c in copies:
        c.start()
    size = out_ref.shape[-1]
    for i, c in enumerate(copies):
        c.wait()
        for slot, head in enumerate(heads):
            out_ref[slot, i] = held[i, :, head * size:(head + 1) * size]
    index.wait()
    groups, tokens = bias_ref.shape
    key_group = lax.broadcasted_iota(jnp.int32, (1, tokens), 1) // (tokens // groups)
    for group in range(groups):
        seen = key_group == group
        for p in range(groups):
            seen |= (key_group == p) & (spans[p] == spans[group] - 1)
        bias_ref[group:group + 1] = jnp.where(seen, 0.0, MASKED)


def attend_kernel(groups, span_ref, in_ref, out_ref):
    slots, _, rows, size = in_ref.shape
    per = slots // groups
    tokens = per * rows
    scale = size ** -0.5

    def piece(part, group):
        block = in_ref[pl.ds(group * per, per), part].astype(jnp.float32)
        return block.reshape(tokens, size).astype(jnp.bfloat16)

    def one(group, carry):
        mine = span_ref[group]
        source = jnp.int32(0)
        found = jnp.int32(0)
        for p in range(groups):
            hit = (span_ref[p] == mine - 1).astype(jnp.int32)
            source = source + hit * p
            found = found + hit
        has = found > 0
        q = piece(0, group)
        dims = (((1,), (1,)), ((), ()))
        own = lax.dot_general(q, piece(1, group), dims, preferred_element_type=jnp.float32) * scale
        before = lax.dot_general(q, piece(1, source), dims, preferred_element_type=jnp.float32) * scale
        before = jnp.where(has, before, -1e30)
        top = jnp.maximum(jnp.max(own, -1, keepdims=True), jnp.max(before, -1, keepdims=True))
        own_w = jnp.exp(own - top)
        before_w = jnp.where(has, jnp.exp(before - top), 0.0)
        total = jnp.sum(own_w, -1, keepdims=True) + jnp.sum(before_w, -1, keepdims=True)
        acc = jnp.dot(own_w.astype(jnp.bfloat16), piece(2, group), preferred_element_type=jnp.float32)
        acc += jnp.dot(before_w.astype(jnp.bfloat16), piece(2, source), preferred_element_type=jnp.float32)
        result = (acc / total).reshape(per, rows, size).astype(jnp.bfloat16)
        out_ref[pl.ds(group * per, per)] = result
        return carry

    lax.fori_loop(0, groups, one, 0)


def attend_pair_kernel(bias_ref, in_ref, out_ref):
    slots, _, rows, size = in_ref.shape
    half = slots * rows // 2

    def piece(part):
        return in_ref[:, part].reshape(-1, size)

    scores = lax.dot_general(
        piece(0), piece(1), (((1,), (1,)), ((), ())), preferred_element_type=jnp.float32
    )
    scores = jnp.concatenate([scores[:half] + bias_ref[0:1], scores[half:] + bias_ref[1:2]], 0)
    scale = size ** -0.5 * math.log2(math.e)
    weights = jnp.exp2((scores - jnp.max(scores, -1, keepdims=True)) * scale)
    share = 1.0 / jnp.sum(weights, -1, keepdims=True)
    acc = jnp.dot(weights.astype(jnp.bfloat16), piece(2), preferred_element_type=jnp.float32)
    out_ref[...] = (acc * share).reshape(slots, rows, size).astype(jnp.bfloat16)


def unpack_kernel(places, in_ref, out_ref):
    size = in_ref.shape[-1]
    for head, slot in enumerate(places):
        out_ref[0, :, head * size:(head + 1) * size] = in_ref[slot]


def shards(groups, ranks, queries, keys, values, span_index):
    rows, width = queries.shape[1:]
    size = width // HEADS
    slots = groups * ranks
    heads, places = slot_heads(slots)
    order = [rank_order(groups, ranks)] if ranks % 4 == 0 else None
    vmem = pl.BlockSpec(memory_space=pltpu.VMEM)
    smem = pl.BlockSpec(memory_space=pltpu.SMEM)
    hbm = pl.BlockSpec(memory_space=pltpu.HBM)
    queries, keys, values = [
        pltpu.with_memory_space_constraint(a, pltpu.HBM) for a in (queries, keys, values)
    ]
    params = pltpu.CompilerParams(vmem_limit_bytes=32 * 2**20)
    span_index = pltpu.with_memory_space_constraint(span_index, pltpu.HBM)
    packed, bias = pl.pallas_call(
        functools.partial(pack_kernel, heads),
        out_shape=[
            jax.ShapeDtypeStruct((slots, 3, rows, size), jnp.bfloat16),
            jax.ShapeDtypeStruct((groups, slots * rows), jnp.float32),
        ],
        in_specs=[hbm] * 4,
        out_specs=[vmem] * 2,
        scratch_shapes=[
            pltpu.VMEM((3, rows, width), jnp.bfloat16),
            pltpu.SMEM((groups,), jnp.int32),
            pltpu.SemaphoreType.DMA((4,)),
        ],
        compiler_params=params,
    )(queries, keys, values, span_index)
    whole = lax.all_to_all(packed, AXES, 0, 0, axis_index_groups=order, tiled=True)
    pair = groups == 2
    done = pl.pallas_call(
        attend_pair_kernel if pair else functools.partial(attend_kernel, groups),
        out_shape=jax.ShapeDtypeStruct((slots, rows, size), jnp.bfloat16),
        in_specs=[vmem if pair else smem, vmem],
        out_specs=vmem,
        compiler_params=params,
    )(bias if pair else span_index, whole)
    back = lax.all_to_all(done, AXES, 0, 0, axis_index_groups=order, tiled=True)
    return pl.pallas_call(
        functools.partial(unpack_kernel, places),
        out_shape=jax.ShapeDtypeStruct((1, rows, width), jnp.bfloat16),
        in_specs=[vmem],
        out_specs=vmem,
        compiler_params=params,
    )(back)


def solution(mesh):
    spec = P("span", "seq", None)
    body = functools.partial(shards, mesh.shape["span"], mesh.shape["seq"])
    return jax.shard_map(body, mesh=mesh, in_specs=(spec, spec, spec, P()), out_specs=spec, check_vma=False)
```

profile of v0, /device:TPU:0, one launch (start us, length us, event | category | flops | bytes accessed | tf_op | source)
XLA Modules:
  0.0 27.5 jit_solution(10869298595379754656)
XLA Ops:
  0.0 0.9 %shard_map.46 = (bf16[32,3,8,128]{3,2,1,0:T(8,128)(2,1)S(1)}, f32[2,256]{1,0:T(2,128)S(1)}) custom-call(bf16[1,8,2560]{2,1,0:T(8,128)(2,1)} %q_hbm.1, bf16[1,8,2560]{2,1,0:T(8,128)(2,1)} %k_hbm.1, bf16[1,8,2560]{2,1,0:T(8,128)(2,1)} %v_hbm.1, s32[2]{0:T(128)} %span_hbm.1), custom_call_target="tpu_custom_call" | custom-call | tf_op jit(solution)/shard_map/pallas_call | solution.py:128
  0.9 16.3 %all_to_all.10.in_ref = bf16[32,3,8,128]{3,2,1,0:T(8,128)(2,1)S(1)} all-to-all(bf16[32,3,8,128]{3,2,1,0:T(8,128)(2,1)S(1)} %get-tuple-element.8), channel_id=1, replica_groups={{0,4,8,12,2,6,10,14,1,5,9,13,3,7,11,15,16,20,24,28,18,22,26,30,17,21,25..., dimensions={0} | all-to-all | bytes 393216 | tf_op jit(solution)/shard_map/all_to_all | solution.py:143
  17.1 0.4 %shard_map.47 = bf16[32,8,128]{2,1,0:T(8,128)(2,1)S(1)} custom-call(f32[2,256]{1,0:T(2,128)S(1)} %get-tuple-element.7.bias_ref, bf16[32,3,8,128]{3,2,1,0:T(8,128)(2,1)S(1)} %all_to_all.10.in_ref), custom_call_target="tpu_custom_call" | custom-call | tf_op jit(solution)/shard_map/pallas_call | solution.py:145
  17.6 9.3 %all_to_all.11.in_ref = bf16[32,8,128]{2,1,0:T(8,128)(2,1)S(1)} all-to-all(bf16[32,8,128]{2,1,0:T(8,128)(2,1)S(1)} %shard_map.47), channel_id=1, replica_groups={{0,4,8,12,2,6,10,14,1,5,9,13,3,7,11,15,16,20,24,28,18,22,26,30,17,21,25..., dimensions={0} | all-to-all | bytes 131072 | tf_op jit(solution)/shard_map/all_to_all | solution.py:152
  26.9 0.6 %shard_map.48 = bf16[1,8,2560]{2,1,0:T(8,128)(2,1)} custom-call(bf16[32,8,128]{2,1,0:T(8,128)(2,1)S(1)} %all_to_all.11.in_ref), custom_call_target="tpu_custom_call" | custom-call | tf_op jit(solution)/shard_map/pallas_call | solution.py:153
where the time goes:
time: 27.7 us; the launch traced here: 27.5 us
  blocking collectives  25.6 us (92%)
  Pallas kernels  1.93 us (7%)
    all_to_all x1, blocking collectives, shards(): lax.all_to_all(packed, AXES, 0, 0, axis_index_groups=order, tiled=True)  16.3 us
    all_to_all x1, blocking collectives, shards(): back = lax.all_to_all(done, AXES, 0, 0, axis_index_groups=order, tiled=True)  9.34 us
    pallas_call x1, Pallas kernels, shards(): pl.pallas_call(functools.partial(pack_kernel, heads), out_shape=[jax.Shap...  0.88 us
    pallas_call x1, Pallas kernels, shards(): pl.pallas_call(functools.partial(unpack_kernel, places), out_shape=jax.Sh...  0.62 us

commit v1 on v0

--- a/solution.py
+++ b/solution.py
@@ -13,33 +13,26 @@
 AXES = ("span", "seq")
 
 
-def slot_heads(slots):
-    spread = [d for d in range(slots) if d % 2 == 0] + [d for d in range(slots) if d % 2]
-    heads = [0] * slots
-    for place, d in enumerate(spread):
-        heads[d] = place % HEADS
-    return heads, spread[:HEADS]
-
-
 def rank_order(groups, ranks):
     per = [r for c in range(2) for y in range(2) for r in range(ranks) if r % 4 == 2 * y + c]
     return [g * ranks + r for g in range(groups) for r in per]
 
 
-def pack_kernel(heads, q_hbm, k_hbm, v_hbm, span_hbm, out_ref, bias_ref, held, spans, sems):
-    copies = [
-        pltpu.make_async_copy(src, held.at[pl.ds(i, 1)], sems.at[i])
-        for i, src in enumerate((q_hbm, k_hbm, v_hbm))
-    ]
-    index = pltpu.make_async_copy(span_hbm, spans, sems.at[3])
-    index.start()
+def pack_kernel(q_hbm, k_hbm, v_hbm, span_hbm, out_ref, bias_ref, spans, sems, span_sem):
+    slots = out_ref.shape[0]
+    copies = []
+    for i, src in enumerate((q_hbm, k_hbm, v_hbm)):
+        for n, first in enumerate(range(0, slots, HEADS)):
+            count = min(HEADS, slots - first)
+            copies.append(
+                pltpu.make_async_copy(
+                    src.at[pl.ds(0, count)], out_ref.at[pl.ds(first, count), i], sems.at[i, n]
+                )
+            )
+    index = pltpu.make_async_copy(span_hbm, spans, span_sem)
     for c in copies:
         c.start()
-    size = out_ref.shape[-1]
-    for i, c in enumerate(copies):
-        c.wait()
-        for slot, head in enumerate(heads):
-            out_ref[slot, i] = held[i, :, head * size:(head + 1) * size]
+    index.start()
     index.wait()
     groups, tokens = bias_ref.shape
     key_group = lax.broadcasted_iota(jnp.int32, (1, tokens), 1) // (tokens // groups)
@@ -48,6 +41,8 @@
         for p in range(groups):
             seen |= (key_group == p) & (spans[p] == spans[group] - 1)
         bias_ref[group:group + 1] = jnp.where(seen, 0.0, MASKED)
+    for c in copies:
+        c.wait()
 
 
 def attend_kernel(groups, span_ref, in_ref, out_ref):
@@ -105,28 +100,31 @@
     out_ref[...] = (acc * share).reshape(slots, rows, size).astype(jnp.bfloat16)
 
 
-def unpack_kernel(places, in_ref, out_ref):
-    size = in_ref.shape[-1]
-    for head, slot in enumerate(places):
-        out_ref[0, :, head * size:(head + 1) * size] = in_ref[slot]
+def unpack_kernel(in_ref, out_hbm, sem):
+    copy = pltpu.make_async_copy(in_ref.at[pl.ds(0, HEADS)], out_hbm, sem)
+    copy.start()
+    copy.wait()
+
+
+def by_head(x):
+    return x.reshape(x.shape[1], HEADS, -1).transpose(1, 0, 2)
 
 
 def shards(groups, ranks, queries, keys, values, span_index):
     rows, width = queries.shape[1:]
     size = width // HEADS
     slots = groups * ranks
-    heads, places = slot_heads(slots)
     order = [rank_order(groups, ranks)] if ranks % 4 == 0 else None
     vmem = pl.BlockSpec(memory_space=pltpu.VMEM)
     smem = pl.BlockSpec(memory_space=pltpu.SMEM)
     hbm = pl.BlockSpec(memory_space=pltpu.HBM)
     queries, keys, values = [
-        pltpu.with_memory_space_constraint(a, pltpu.HBM) for a in (queries, keys, values)
+        pltpu.with_memory_space_constraint(by_head(a), pltpu.HBM) for a in (queries, keys, values)
     ]
     params = pltpu.CompilerParams(vmem_limit_bytes=32 * 2**20)
     span_index = pltpu.with_memory_space_constraint(span_index, pltpu.HBM)
     packed, bias = pl.pallas_call(
-        functools.partial(pack_kernel, heads),
+        pack_kernel,
         out_shape=[
             jax.ShapeDtypeStruct((slots, 3, rows, size), jnp.bfloat16),
             jax.ShapeDtypeStruct((groups, slots * rows), jnp.float32),
@@ -134,9 +132,9 @@
         in_specs=[hbm] * 4,
         out_specs=[vmem] * 2,
         scratch_shapes=[
-            pltpu.VMEM((3, rows, width), jnp.bfloat16),
             pltpu.SMEM((groups,), jnp.int32),
-            pltpu.SemaphoreType.DMA((4,)),
+            pltpu.SemaphoreType.DMA((3, -(-slots // HEADS))),
+            pltpu.SemaphoreType.DMA(()),
         ],
         compiler_params=params,
     )(queries, keys, values, span_index)
@@ -150,13 +148,15 @@
         compiler_params=params,
     )(bias if pair else span_index, whole)
     back = lax.all_to_all(done, AXES, 0, 0, axis_index_groups=order, tiled=True)
-    return pl.pallas_call(
-        functools.partial(unpack_kernel, places),
-        out_shape=jax.ShapeDtypeStruct((1, rows, width), jnp.bfloat16),
+    result = pl.pallas_call(
+        unpack_kernel,
+        out_shape=jax.ShapeDtypeStruct((HEADS, rows, size), jnp.bfloat16),
         in_specs=[vmem],
-        out_specs=vmem,
+        out_specs=hbm,
+        scratch_shapes=[pltpu.SemaphoreType.DMA(())],
         compiler_params=params,
     )(back)
+    return result.transpose(1, 0, 2).reshape(1, rows, width)
 
 
 def solution(mesh):

time: 27.7 us -> 27.8 us (level)
  no operation moved by 1% of the time
where the time goes in v1:
time: 27.8 us; the launch traced here: 27.6 us
  blocking collectives  25.6 us (92%)
  Pallas kernels  1.96 us (7%)
    all_to_all x1, blocking collectives, shards(): lax.all_to_all(packed, AXES, 0, 0, axis_index_groups=order, tiled=True)  16.3 us
    all_to_all x1, blocking collectives, shards(): back = lax.all_to_all(done, AXES, 0, 0, axis_index_groups=order, tiled=True)  9.34 us
    pallas_call x1, Pallas kernels, shards(): pl.pallas_call(pack_kernel, out_shape=[jax.ShapeDtypeStruct((slots, 3, ro...  0.91 us
    pallas_call x1, Pallas kernels, shards(): pl.pallas_call(unpack_kernel, out_shape=jax.ShapeDtypeStruct((HEADS, rows...  0.62 us

profile of v1, /device:TPU:0, one launch (start us, length us, event | category | flops | bytes accessed | tf_op | source)
XLA Modules:
  0.0 27.6 jit_solution(4740163779798918766)
XLA Ops:
  0.0 0.9 %shard_map.46 = (bf16[32,3,8,128]{3,2,1,0:T(8,128)(2,1)S(1)}, f32[2,256]{1,0:T(2,128)S(1)}) custom-call(bf16[20,8,128]{2,1,0:T(8,128)(2,1)} %bitcast.12, bf16[20,8,128]{2,1,0:T(8,128)(2,1)} %bitcast.13, bf16[20,8,128]{2,1,0:T(8,128)(2,1)} %bitcast.14, s32[2]{0:T(128)} %span_hbm.1), custom_call_target="tpu_custom_call" | custom-call | tf_op jit(solution)/shard_map/pallas_call | solution.py:126
  0.9 16.3 %all_to_all.10.in_ref = bf16[32,3,8,128]{3,2,1,0:T(8,128)(2,1)S(1)} all-to-all(bf16[32,3,8,128]{3,2,1,0:T(8,128)(2,1)S(1)} %get-tuple-element.8), channel_id=1, replica_groups={{0,4,8,12,2,6,10,14,1,5,9,13,3,7,11,15,16,20,24,28,18,22,26,30,17,21,25..., dimensions={0} | all-to-all | bytes 393216 | tf_op jit(solution)/shard_map/all_to_all | solution.py:141
  17.2 0.4 %shard_map.47 = bf16[32,8,128]{2,1,0:T(8,128)(2,1)S(1)} custom-call(f32[2,256]{1,0:T(2,128)S(1)} %get-tuple-element.7.bias_ref, bf16[32,3,8,128]{3,2,1,0:T(8,128)(2,1)S(1)} %all_to_all.10.in_ref), custom_call_target="tpu_custom_call" | custom-call | tf_op jit(solution)/shard_map/pallas_call | solution.py:143
  17.6 9.3 %all_to_all.11.in_ref = bf16[32,8,128]{2,1,0:T(8,128)(2,1)S(1)} all-to-all(bf16[32,8,128]{2,1,0:T(8,128)(2,1)S(1)} %shard_map.47), channel_id=1, replica_groups={{0,4,8,12,2,6,10,14,1,5,9,13,3,7,11,15,16,20,24,28,18,22,26,30,17,21,25..., dimensions={0} | all-to-all | bytes 131072 | tf_op jit(solution)/shard_map/all_to_all | solution.py:150
  26.9 0.6 %shard_map.48 = bf16[20,8,128]{2,1,0:T(8,128)(2,1)} custom-call(bf16[32,8,128]{2,1,0:T(8,128)(2,1)S(1)} %all_to_all.11.in_ref), custom_call_target="tpu_custom_call" | custom-call | tf_op jit(solution)/shard_map/pallas_call | solution.py:151

commit v2 on v0

--- a/solution.py
+++ b/solution.py
@@ -26,13 +26,11 @@
     return [g * ranks + r for g in range(groups) for r in per]
 
 
-def pack_kernel(heads, q_hbm, k_hbm, v_hbm, span_hbm, out_ref, bias_ref, held, spans, sems):
+def pack_kernel(heads, q_hbm, k_hbm, v_hbm, out_ref, held, sems):
     copies = [
         pltpu.make_async_copy(src, held.at[pl.ds(i, 1)], sems.at[i])
         for i, src in enumerate((q_hbm, k_hbm, v_hbm))
     ]
-    index = pltpu.make_async_copy(span_hbm, spans, sems.at[3])
-    index.start()
     for c in copies:
         c.start()
     size = out_ref.shape[-1]
@@ -40,14 +38,6 @@
         c.wait()
         for slot, head in enumerate(heads):
             out_ref[slot, i] = held[i, :, head * size:(head + 1) * size]
-    index.wait()
-    groups, tokens = bias_ref.shape
-    key_group = lax.broadcasted_iota(jnp.int32, (1, tokens), 1) // (tokens // groups)
-    for group in range(groups):
-        seen = key_group == group
-        for p in range(groups):
-            seen |= (key_group == p) & (spans[p] == spans[group] - 1)
-        bias_ref[group:group + 1] = jnp.where(seen, 0.0, MASKED)
 
 
 def attend_kernel(groups, span_ref, in_ref, out_ref):
@@ -87,7 +77,7 @@
     lax.fori_loop(0, groups, one, 0)
 
 
-def attend_pair_kernel(bias_ref, in_ref, out_ref):
+def attend_pair_kernel(span_ref, in_ref, out_ref):
     slots, _, rows, size = in_ref.shape
     half = slots * rows // 2
 
@@ -97,7 +87,13 @@
     scores = lax.dot_general(
         piece(0), piece(1), (((1,), (1,)), ((), ())), preferred_element_type=jnp.float32
     )
-    scores = jnp.concatenate([scores[:half] + bias_ref[0:1], scores[half:] + bias_ref[1:2]], 0)
+    spans = span_ref[...].reshape(1, 2)
+    key_group = lax.broadcasted_iota(jnp.int32, (1, slots * rows), 1) // half
+    bias = [
+        jnp.where((key_group == group) | (spans[:, group:group + 1] == 1), 0.0, MASKED)
+        for group in range(2)
+    ]
+    scores = jnp.concatenate([scores[:half] + bias[0], scores[half:] + bias[1]], 0)
     scale = size ** -0.5 * math.log2(math.e)
     weights = jnp.exp2((scores - jnp.max(scores, -1, keepdims=True)) * scale)
     share = 1.0 / jnp.sum(weights, -1, keepdims=True)
@@ -124,22 +120,14 @@
         pltpu.with_memory_space_constraint(a, pltpu.HBM) for a in (queries, keys, values)
     ]
     params = pltpu.CompilerParams(vmem_limit_bytes=32 * 2**20)
-    span_index = pltpu.with_memory_space_constraint(span_index, pltpu.HBM)
-    packed, bias = pl.pallas_call(
+    packed = pl.pallas_call(
         functools.partial(pack_kernel, heads),
-        out_shape=[
-            jax.ShapeDtypeStruct((slots, 3, rows, size), jnp.bfloat16),
-            jax.ShapeDtypeStruct((groups, slots * rows), jnp.float32),
-        ],
-        in_specs=[hbm] * 4,
-        out_specs=[vmem] * 2,
-        scratch_shapes=[
-            pltpu.VMEM((3, rows, width), jnp.bfloat16),
-            pltpu.SMEM((groups,), jnp.int32),
-            pltpu.SemaphoreType.DMA((4,)),
-        ],
+        out_shape=jax.ShapeDtypeStruct((slots, 3, rows, size), jnp.bfloat16),
+        in_specs=[hbm] * 3,
+        out_specs=vmem,
+        scratch_shapes=[pltpu.VMEM((3, rows, width), jnp.bfloat16), pltpu.SemaphoreType.DMA((3,))],
         compiler_params=params,
-    )(queries, keys, values, span_index)
+    )(queries, keys, values)
     whole = lax.all_to_all(packed, AXES, 0, 0, axis_index_groups=order, tiled=True)
     pair = groups == 2
     done = pl.pallas_call(
@@ -148,7 +136,7 @@
         in_specs=[vmem if pair else smem, vmem],
         out_specs=vmem,
         compiler_params=params,
-    )(bias if pair else span_index, whole)
+    )(span_index, whole)
     back = lax.all_to_all(done, AXES, 0, 0, axis_index_groups=order, tiled=True)
     return pl.pallas_call(
         functools.partial(unpack_kernel, places),

time: 27.7 us -> 27.7 us (level)
  no operation moved by 1% of the time
where the time goes in v2:
time: 27.7 us; the launch traced here: 27.5 us
  blocking collectives  25.6 us (92%)
  Pallas kernels  1.89 us (7%)
    all_to_all x1, blocking collectives, shards(): lax.all_to_all(packed, AXES, 0, 0, axis_index_groups=order, tiled=True)  16.3 us
    all_to_all x1, blocking collectives, shards(): back = lax.all_to_all(done, AXES, 0, 0, axis_index_groups=order, tiled=True)  9.34 us
    pallas_call x1, Pallas kernels, shards(): pl.pallas_call(functools.partial(pack_kernel, heads), out_shape=jax.Shape...  0.85 us
    pallas_call x1, Pallas kernels, shards(): pl.pallas_call(functools.partial(unpack_kernel, places), out_shape=jax.Sh...  0.62 us

profile of v2, /device:TPU:0, one launch (start us, length us, event | category | flops | bytes accessed | tf_op | source)
XLA Modules:
  0.0 27.5 jit_solution(5419412432155230778)
XLA Ops:
  0.0 0.9 %shard_map.46 = bf16[32,3,8,128]{3,2,1,0:T(8,128)(2,1)S(1)} custom-call(bf16[1,8,2560]{2,1,0:T(8,128)(2,1)} %q_hbm.1, bf16[1,8,2560]{2,1,0:T(8,128)(2,1)} %k_hbm.1, bf16[1,8,2560]{2,1,0:T(8,128)(2,1)} %v_hbm.1), custom_call_target="tpu_custom_call" | custom-call | tf_op jit(solution)/shard_map/pallas_call | solution.py:123
  0.9 0.0 copy-start
  0.9 16.3 %all_to_all.10.in_ref = bf16[32,3,8,128]{3,2,1,0:T(8,128)(2,1)S(1)} all-to-all(bf16[32,3,8,128]{3,2,1,0:T(8,128)(2,1)S(1)} %shard_map.46), channel_id=1, replica_groups={{0,4,8,12,2,6,10,14,1,5,9,13,3,7,11,15,16,20,24,28,18,22,26,30,17,21,25..., dimensions={0} | all-to-all | bytes 393216 | tf_op jit(solution)/shard_map/all_to_all | solution.py:131
  17.1 0.0 copy-done
  17.1 0.4 %shard_map.47 = bf16[32,8,128]{2,1,0:T(8,128)(2,1)S(1)} custom-call(s32[2]{0:T(128)S(1)} %copy-done, bf16[32,3,8,128]{3,2,1,0:T(8,128)(2,1)S(1)} %all_to_all.10.in_ref), custom_call_target="tpu_custom_call" | custom-call | tf_op jit(solution)/shard_map/pallas_call | solution.py:133
  17.6 9.3 %all_to_all.11.in_ref = bf16[32,8,128]{2,1,0:T(8,128)(2,1)S(1)} all-to-all(bf16[32,8,128]{2,1,0:T(8,128)(2,1)S(1)} %shard_map.47), channel_id=1, replica_groups={{0,4,8,12,2,6,10,14,1,5,9,13,3,7,11,15,16,20,24,28,18,22,26,30,17,21,25..., dimensions={0} | all-to-all | bytes 131072 | tf_op jit(solution)/shard_map/all_to_all | solution.py:140
  26.9 0.6 %shard_map.48 = bf16[1,8,2560]{2,1,0:T(8,128)(2,1)} custom-call(bf16[32,8,128]{2,1,0:T(8,128)(2,1)S(1)} %all_to_all.11.in_ref), custom_call_target="tpu_custom_call" | custom-call | tf_op jit(solution)/shard_map/pallas_call | solution.py:141
Async XLA Ops:
  0.9 16.3 %copy-start = (s32[2]{0:T(128)S(1)}, s32[2]{0:T(128)}, u32[]{:S(2)}) copy-start(s32[2]{0:T(128)} %span_ref.1) | copy-start | bytes 28

commit v3 on v2

--- a/solution.py
+++ b/solution.py
@@ -32,7 +32,7 @@
         for i, src in enumerate((q_hbm, k_hbm, v_hbm))
     ]
     for c in copies:
-        c.start()
+        c.start(priority=1 if c is copies[1] else 0)
     size = out_ref.shape[-1]
     for i, c in enumerate(copies):
         c.wait()

time: 27.7 us -> 27.7 us (level)
  no operation moved by 1% of the time
where the time goes in v3:
time: 27.7 us; the launch traced here: 27.5 us
  blocking collectives  25.6 us (92%)
  Pallas kernels  1.9 us (7%)
    all_to_all x1, blocking collectives, shards(): lax.all_to_all(packed, AXES, 0, 0, axis_index_groups=order, tiled=True)  16.3 us
    all_to_all x1, blocking collectives, shards(): back = lax.all_to_all(done, AXES, 0, 0, axis_index_groups=order, tiled=True)  9.34 us
    pallas_call x1, Pallas kernels, shards(): pl.pallas_call(functools.partial(pack_kernel, heads), out_shape=jax.Shape...  0.86 us
    pallas_call x1, Pallas kernels, shards(): pl.pallas_call(functools.partial(unpack_kernel, places), out_shape=jax.Sh...  0.62 us

profile of v3, /device:TPU:0, one launch (start us, length us, event | category | flops | bytes accessed | tf_op | source)
XLA Modules:
  0.0 27.5 jit_solution(7708654542841238568)
XLA Ops:
  0.0 0.9 %shard_map.46 = bf16[32,3,8,128]{3,2,1,0:T(8,128)(2,1)S(1)} custom-call(bf16[1,8,2560]{2,1,0:T(8,128)(2,1)} %q_hbm.1, bf16[1,8,2560]{2,1,0:T(8,128)(2,1)} %k_hbm.1, bf16[1,8,2560]{2,1,0:T(8,128)(2,1)} %v_hbm.1), custom_call_target="tpu_custom_call" | custom-call | tf_op jit(solution)/shard_map/pallas_call | solution.py:123
  0.9 0.0 copy-start
  0.9 16.3 %all_to_all.10.in_ref = bf16[32,3,8,128]{3,2,1,0:T(8,128)(2,1)S(1)} all-to-all(bf16[32,3,8,128]{3,2,1,0:T(8,128)(2,1)S(1)} %shard_map.46), channel_id=1, replica_groups={{0,4,8,12,2,6,10,14,1,5,9,13,3,7,11,15,16,20,24,28,18,22,26,30,17,21,25..., dimensions={0} | all-to-all | bytes 393216 | tf_op jit(solution)/shard_map/all_to_all | solution.py:131
  17.1 0.0 copy-done
  17.1 0.4 %shard_map.47 = bf16[32,8,128]{2,1,0:T(8,128)(2,1)S(1)} custom-call(s32[2]{0:T(128)S(1)} %copy-done, bf16[32,3,8,128]{3,2,1,0:T(8,128)(2,1)S(1)} %all_to_all.10.in_ref), custom_call_target="tpu_custom_call" | custom-call | tf_op jit(solution)/shard_map/pallas_call | solution.py:133
  17.6 9.3 %all_to_all.11.in_ref = bf16[32,8,128]{2,1,0:T(8,128)(2,1)S(1)} all-to-all(bf16[32,8,128]{2,1,0:T(8,128)(2,1)S(1)} %shard_map.47), channel_id=1, replica_groups={{0,4,8,12,2,6,10,14,1,5,9,13,3,7,11,15,16,20,24,28,18,22,26,30,17,21,25..., dimensions={0} | all-to-all | bytes 131072 | tf_op jit(solution)/shard_map/all_to_all | solution.py:140
  26.9 0.6 %shard_map.48 = bf16[1,8,2560]{2,1,0:T(8,128)(2,1)} custom-call(bf16[32,8,128]{2,1,0:T(8,128)(2,1)S(1)} %all_to_all.11.in_ref), custom_call_target="tpu_custom_call" | custom-call | tf_op jit(solution)/shard_map/pallas_call | solution.py:141
Async XLA Ops:
  0.9 16.3 %copy-start = (s32[2]{0:T(128)S(1)}, s32[2]{0:T(128)}, u32[]{:S(2)}) copy-start(s32[2]{0:T(128)} %span_ref.1) | copy-start | bytes 28
